TPU v7x, 32 devices: a whole 2x2x4 slice. The times are simulated.
32 devices in a mesh: dp: 16 (over z, x, core), expert: 2 (over y).
Axes of the slice: x: 2, y: 2, z: 4, core: 2. Of those that a mesh axis runs over, the one named last changes fastest.
Arguments:
- acts: bfloat16 [8192, 8, 1024], P(('dp', 'expert')), may hold values from -6 to 6
- grads: bfloat16 [8192, 2048], P(('dp', 'expert')), may hold values from -6 to 6
- probs: float32 [8192, 8], P(('dp', 'expert')), may hold values from 0.02 to 0.3
- expert_ids: int32 [8192, 8], P(('dp', 'expert')), may hold values from 0 to 63, as said below
- example_ids: int32 [16, 512], P('dp', 'expert'), may hold values from 0 to 2, never falling along the last dimension, each value on 1 to 256 neighbouring positions
- act_basis: bfloat16 [2, 1024, 1024], P('expert', 'dp'), may hold values from -0.1875 to 0.1875
- grad_basis: bfloat16 [2, 2048, 2048], P('expert', 'dp'), may hold values from -0.125 to 0.125
Outputs:
- eigenvalues: float32 [2, 1024, 2048], P('expert', 'dp')
Inputs may be any that keep to these rules, and one draw needn't show every extreme that they name: `expert_ids`: each token names 8 different experts. Experts 0 to 1 form the window. Among the 256 tokens of one device every window expert is named by at least one and at most 64 tokens, and one window expert, the same for all devices, is named by exactly 64 tokens of every device.
All inputs are finite; a program needn't handle non-finite values.
Results may differ from a plain program's by a relative error of at most 0.004.
Values may be sent and summed in bfloat16 or wider, within the bound.
A program may use at most 64 MiB of HBM per device.

v0:
```python
import math

import jax
import jax.numpy as jnp
from jax import lax
from jax.sharding import PartitionSpec as P

EXAMPLES = 3


def route_block(picked, activity, weights, gradient, labels, expert):
    count_tok = picked.shape[0]
    count_slot = picked.shape[1]
    capacity = count_tok // 4
    names = (picked == expert).astype(jnp.int32)
    named = jnp.sum(names, axis=1, dtype=jnp.int32)
    which = jnp.sum(
        names * jnp.arange(count_slot, dtype=jnp.int32)[None, :], axis=1, dtype=jnp.int32
    )
    ranked = jnp.cumsum(named, dtype=jnp.int32) - 1
    places = jnp.arange(capacity, dtype=jnp.int32)
    table = ((ranked[None, :] == places[:, None]) & (named[None, :] == 1)).astype(jnp.int32)
    token = jnp.sum(
        table * jnp.arange(count_tok, dtype=jnp.int32)[None, :], axis=1, dtype=jnp.int32
    )
    filled = jnp.sum(table, axis=1, dtype=jnp.int32)
    flat_index = token * count_slot + which[token]
    rows_acts = activity.reshape(count_tok * count_slot, activity.shape[-1])[flat_index] * filled[
        :, None
    ].astype(activity.dtype)
    scaled = weights.reshape(count_tok * count_slot)[flat_index] * filled.astype(weights.dtype)
    rows_grads = (scaled[:, None] * gradient[token].astype(jnp.float32)).astype(jnp.bfloat16)
    example_range = jnp.arange(EXAMPLES, dtype=jnp.int32)
    member = ((labels[token][:, None] == example_range[None, :]) & (filled[:, None] == 1)).astype(
        jnp.bfloat16
    )
    return (rows_acts, rows_grads, member)


def body(acts, grads, probs, expert_ids, example_ids, act_basis, grad_basis):
    owners = lax.axis_size("expert")
    shards = lax.axis_size("dp")
    hidden_width = acts.shape[2]
    model_width = grads.shape[1]
    labels = example_ids[0]
    experts = jnp.arange(owners, dtype=jnp.int32)

    def route_one(expert):
        return route_block(expert_ids, acts, probs, grads, labels, expert)

    send_acts, send_grads, send_member = jax.vmap(route_one)(experts)
    got_acts, got_grads, got_member = (
        lax.all_to_all(send_acts, "expert", split_axis=0, concat_axis=0, tiled=True),
        lax.all_to_all(send_grads, "expert", split_axis=0, concat_axis=0, tiled=True),
        lax.all_to_all(send_member, "expert", split_axis=0, concat_axis=0, tiled=True),
    )
    routed_acts = got_acts.reshape(-1, hidden_width)
    routed_grads = got_grads.reshape(-1, model_width)
    member = got_member.reshape(-1, got_member.shape[-1])
    basis_acts = act_basis[0]
    basis_grads = grad_basis[0]
    full_acts, full_grads = (
        lax.all_gather(basis_acts, "dp", axis=0, tiled=True),
        lax.all_gather(basis_grads, "dp", axis=0, tiled=True),
    )
    rotated_acts = jnp.dot(routed_acts, full_acts, preferred_element_type=jnp.float32).astype(
        jnp.bfloat16
    )
    rotated_grads = jnp.dot(routed_grads, full_grads, preferred_element_type=jnp.float32).astype(
        jnp.bfloat16
    )
    scale = 1.0 / (member.shape[-1] * shards)
    member_first = member.T
    width_step = math.gcd(hidden_width, 256)
    pieces = []
    for offset in range(0, hidden_width, width_step):
        columns = lax.dynamic_slice_in_dim(rotated_acts, 0 + offset, width_step, 1)
        masked = member_first[:, :, None] * columns[None, :, :]
        product = jnp.einsum(
            "jrf,rd->jfd", masked, rotated_grads, preferred_element_type=jnp.float32
        )
        pieces.append(jnp.sum(product * product, axis=0))
    totals = jnp.concatenate(pieces, axis=0) * scale
    result = lax.psum_scatter(totals, "dp", scatter_dimension=0, tiled=True)
    return result[None]


def solution(mesh):
    return jax.shard_map(
        body,
        mesh=mesh,
        in_specs=(
            P(("dp", "expert"), None, None),
            P(("dp", "expert"), None),
            P(("dp", "expert"), None),
            P(("dp", "expert"), None),
            P("dp", "expert"),
            P("expert", "dp", None),
            P("expert", "dp", None),
        ),
        out_specs=P("expert", "dp", None),
        check_vma=False,
    )
```

profile of v0, /device:TPU:0, one launch (start us, length us, event | category | flops | bytes accessed | tf_op | source)
XLA Modules:
  0.0 251.8 jit_solution(6031342446633321386)
XLA Ops:
  6.5 0.7 all-gather.5.cloned.1.call-update
  7.3 0.7 all-gather.7.cloned.1.call-update
  8.0 0.7 select_reduce_fusion.1
  8.7 0.6 reduce-window.6
  9.4 0.2 slice_reduce_fusion
  9.6 0.2 reduce-window.9
  9.8 0.2 convert_reduce_fusion
  10.1 1.6 gather_fusion.4
  11.8 1.6 gather_fusion
  13.6 0.6 fusion.28
  14.2 4.2 %all-to-all-start = ((bf16[2,64,3]{1,2,0:T(4,128)(2,1)}), bf16[2,64,3]{1,2,0:T(4,128)(2,1)S(1)}, u32[]{:S(2)}, u32[]{:S(2)}) async-start(bf16[2,64,3]{1,2,0:T(4,128)(2,1)} %fusion.28), calls=%async_computation | async-start | bytes 4096 | tf_op jit(solution)/shard_map/all_to_all | solution.py:55
  18.5 0.8 copy.34
  19.4 1.1 gather_fusion.2
  20.7 3.8 %gather_fusion.1 = bf16[128,1024]{1,0:T(8,128)(2,1)S(1)} fusion(bf16[2048,1024]{1,0:T(8,128)(2,1)} %bitcast.57, s32[1024]{0:T(1024)S(1)} %pad_clamp_fusion), kind=kCustom, calls=%fused_computation.1 | custom fusion | bytes 524800 | tf_op jit(solution)/shard_map/vmap()/gather | solution.py:28
  24.4 0.8 broadcast_multiply_fusion
  25.3 0.9 gather_fusion.3
  26.2 3.5 %all-to-all-start.1 = ((bf16[2,64,1024]{2,1,0:T(8,128)(2,1)}), bf16[2,64,1024]{2,1,0:T(8,128)(2,1)S(1)}, u32[]{:S(2)}, u32[]{:S(2)}) async-start(bf16[2,64,1024]{2,1,0:T(8,128)(2,1)} %broadcast_multiply_fusion), calls=%async_computation.1 | async-start | bytes 524288 | tf_op jit(solution)/shard_map/all_to_all | solution.py:53
  29.7 0.9 fusion.13
  30.7 4.6 %all-to-all-done.1 = bf16[2,64,1024]{2,1,0:T(8,128)(2,1)S(1)} async-done(((bf16[2,64,1024]{2,1,0:T(8,128)(2,1)}), bf16[2,64,1024]{2,1,0:T(8,128)(2,1)S(1)}, u32[]{:S(2)}, u32[]{:S(2)}) %all-to-all-start.1) | async-done | bytes 262176 | tf_op jit(solution)/shard_map/all_to_all | solution.py:53
  35.3 3.5 %all-to-all-start.2 = ((bf16[2,64,2048]{2,1,0:T(8,128)(2,1)}), bf16[2,64,2048]{2,1,0:T(8,128)(2,1)S(1)}, u32[]{:S(2)}, u32[]{:S(2)}) async-start(bf16[2,64,2048]{2,1,0:T(8,128)(2,1)} %fusion.13), calls=%async_computation.2 | async-start | bytes 1048576 | tf_op jit(solution)/shard_map/all_to_all | solution.py:54
  38.9 14.8 %all-gather.5.cloned.1.call-done = bf16[1,1024,1024]{2,1,0:T(8,128)(2,1)} async-done(((bf16[1,64,1024]{2,1,0:T(8,128)(2,1)}), bf16[1,1024,1024]{2,1,0:T(8,128)(2,1)}) %all-gather.5.cloned.1.call-update) | async-done | bytes 2097168 | tf_op jit(solution)/shard_map/all_gather | solution.py:63
  53.7 2.0 fusion.10
  55.9 0.1 copy.37
  56.0 0.1 copy.36
  56.2 73.3 %all-gather.7.cloned.1.call-done = bf16[1,2048,2048]{2,1,0:T(8,128)(2,1)} async-done(((bf16[1,128,2048]{2,1,0:T(8,128)(2,1)}), bf16[1,2048,2048]{2,1,0:T(8,128)(2,1)}) %all-gather.7.cloned.1.call-update) | async-done | bytes 8388624 | tf_op jit(solution)/shard_map/all_gather | solution.py:64
  129.5 4.6 %fusion.5 = bf16[128,2048,1]{1,0,2:T(8,128)(2,1)S(1)} fusion(bf16[128,2048]{1,0:T(8,128)(2,1)S(1)} %bitcast.53, bf16[1,2048,2048]{2,1,0:T(8,128)(2,1)} %all-gather.7.cloned.1.call-done), kind=kOutput, calls=%fused_computation.13 | convolution fusion | flops 1074003968 | bytes 9437184 | tf_op jit(solution)/shard_map/dot_general | solution.py:69
  134.2 1.0 multiply_reduce_fusion
  135.2 1.0 multiply_reduce_fusion.1
  136.1 1.0 multiply_reduce_fusion.2
  137.1 1.0 multiply_reduce_fusion.3
  138.1 4.2 %maximum_multiply_fusion = f32[1024,2048]{1,0:T(8,128)} fusion(f32[256,2048]{1,0:T(8,128)S(1)} %multiply_reduce_fusion, f32[256,2048]{1,0:T(8,128)S(1)} %multiply_reduce_fusion.1, f32[256,2048]{1,0:T(8,128)S(1)} %multiply_reduce_fusion.2, f32[256,2048]{1,0:T(8,128)S(1)} %multiply_reduce_fusion.3), kind=kLoop, calls=%fused_computation.5 | loop fusion | flops 8388608 | bytes 16777216 | tf_op jit(solution)/shard_map/mul | solution.py:83
  142.3 103.0 %reduce-scatter.2.cloned.1.call-done = f32[64,2048]{1,0:T(8,128)} async-done(((f32[1024,2048]{1,0:T(8,128)}), f32[64,2048]{1,0:T(8,128)}) %reduce-scatter.2.cloned.1.call-update) | async-done | bytes 524304 | tf_op jit(solution)/shard_map/reduce_scatter | solution.py:84
  (31 shorter events, 1.2 us)
Async XLA Ops:
  6.5 18.7 %copy-start = (bf16[256,2048]{1,0:T(8,128)(2,1)S(1)}, bf16[256,2048]{1,0:T(8,128)(2,1)}, u32[]{:S(2)}) copy-start(bf16[256,2048]{1,0:T(8,128)(2,1)} %param.8) | copy-start | bytes 3145732
  6.5 47.1 %all-gather.5.cloned.1.call-start = ((), (), s32[]{:S(2)}) async-start(), calls=%async_computation.5 | async-start | bytes 2228224 | tf_op jit(solution)/shard_map/all_gather | solution.py:63
  7.3 122.3 %all-gather.7.cloned.1.call-start = ((), (), s32[]{:S(2)}) async-start(), calls=%async_computation.6 | async-start | bytes 8912896 | tf_op jit(solution)/shard_map/all_gather | solution.py:64
  14.2 12.0 %all-to-all-start = ((bf16[2,64,3]{1,2,0:T(4,128)(2,1)}), bf16[2,64,3]{1,2,0:T(4,128)(2,1)S(1)}, u32[]{:S(2)}, u32[]{:S(2)}) async-start(bf16[2,64,3]{1,2,0:T(4,128)(2,1)} %fusion.28), calls=%async_computation | async-start | bytes 4096 | tf_op jit(solution)/shard_map/all_to_all | solution.py:55
  26.2 9.1 %all-to-all-start.1 = ((bf16[2,64,1024]{2,1,0:T(8,128)(2,1)}), bf16[2,64,1024]{2,1,0:T(8,128)(2,1)S(1)}, u32[]{:S(2)}, u32[]{:S(2)}) async-start(bf16[2,64,1024]{2,1,0:T(8,128)(2,1)} %broadcast_multiply_fusion), calls=%async_computation.1 | async-start | bytes 524288 | tf_op jit(solution)/shard_map/all_to_all | solution.py:53
  35.3 20.9 %all-to-all-start.2 = ((bf16[2,64,2048]{2,1,0:T(8,128)(2,1)}), bf16[2,64,2048]{2,1,0:T(8,128)(2,1)S(1)}, u32[]{:S(2)}, u32[]{:S(2)}) async-start(bf16[2,64,2048]{2,1,0:T(8,128)(2,1)} %fusion.13), calls=%async_computation.2 | async-start | bytes 1048576 | tf_op jit(solution)/shard_map/all_to_all | solution.py:54
  38.8 206.4 %reduce-scatter.2.cloned.1.call-start = ((), (), s32[]{:S(2)}) async-start(), calls=%async_computation.4 | async-start | bytes 8912896 | tf_op jit(solution)/shard_map/reduce_scatter | solution.py:84
Sparse Core Ops, SparseCore 0:
  9.5 44.1 all-gather.4
  55.8 73.6 all-gather.6
  142.4 102.8 reduce-scatter.1
where the time goes:
time: 252 us
  waiting for transfers between devices  197 us (78%)
  between operations  13.3 us (5%)
  local copies, waits for them, and re-layouts  11.3 us (4%)
  starting transfers between devices  11.3 us (4%)
  matrix products  10.5 us (4%)
  other arithmetic  8.3 us (3%)
    reduce_scatter x1, waiting for transfers between devices, body(): result = lax.psum_scatter(totals, 'dp', scatter_dimension=0, tiled=True)  103 us
    all_gather x1, waiting for transfers between devices, body(): lax.all_gather(basis_grads, 'dp', axis=0, tiled=True)  73.3 us
    all_gather x1, waiting for transfers between devices, body(): lax.all_gather(basis_acts, 'dp', axis=0, tiled=True)  14.8 us
  transfers between devices with their start and end apart: 6, of which 4 were waited for; matrix products, arithmetic and copies ran while one was open for 7% of the time, Pallas kernels for 0%

commit v1 on v0

--- a/solution.py
+++ b/solution.py
@@ -3,6 +3,8 @@
 import jax
 import jax.numpy as jnp
 from jax import lax
+from jax.experimental import pallas as pl
+from jax.experimental.pallas import tpu as pltpu
 from jax.sharding import PartitionSpec as P
 
 EXAMPLES = 3
@@ -85,9 +87,458 @@
     return result[None]
 
 
+NZ = 4
+CHUNK = 512
+
+
+def kernel(
+    ids_ref, probs_ref, labels_ref, acts_ref, grads_ref, act_basis_ref, grad_basis_ref, out_ref,
+    full_acts, full_grads, send_a, send_g, send_m, rows_a, rows_g, rows_m, masked,
+    acc, core_out, core_in, x_out, x_in, up_out, up_in, down_out, down_in,
+    y_send, y_recv, g_send, g_recv, r_send, r_recv,
+):
+    me = lax.axis_index("dp")
+    own = lax.axis_index("expert")
+    core = lax.rem(me, 2)
+    x = lax.rem(me // 2, 2)
+    z = me // 4
+    chunks = full_grads.shape[0]
+    tall = grad_basis_ref.shape[0]
+    short = act_basis_ref.shape[0]
+    block = out_ref.shape[0]
+    capacity = send_a.shape[0]
+    bf16, f32 = jnp.bfloat16, jnp.float32
+
+    def at(zz, xx, cc):
+        return {"dp": (zz * 2 + xx) * 2 + cc}
+
+    sibling, beside = at(z, x, 1 - core), at(z, 1 - x, core)
+    above, below = at(z + 1, x, core), at(z - 1, x, core)
+    partner = {"expert": 1 - own}
+
+    barrier = pltpu.get_barrier_semaphore()
+    for target in (sibling, beside, partner):
+        pl.semaphore_signal(barrier, inc=1, device_id=target, device_id_type=pl.DeviceIdType.MESH)
+
+    @pl.when(z < NZ - 1)
+    def _():
+        pl.semaphore_signal(barrier, inc=1, device_id=above, device_id_type=pl.DeviceIdType.MESH)
+
+    @pl.when(z > 0)
+    def _():
+        pl.semaphore_signal(barrier, inc=1, device_id=below, device_id_type=pl.DeviceIdType.MESH)
+
+    ends = (z == 0).astype(jnp.int32) + (z == NZ - 1).astype(jnp.int32)
+    pl.semaphore_wait(barrier, 5 - ends)
+
+    def remote(src, dst, ssem, rsem, target):
+        return pltpu.make_async_remote_copy(
+            src_ref=src, dst_ref=dst, send_sem=ssem, recv_sem=rsem,
+            device_id=target, device_id_type=pl.DeviceIdType.MESH,
+        )
+
+    def shard(part, zz, xx, cc):
+        index = (zz * 2 + xx) * 2 + cc
+        if part == 0:
+            return full_acts.at[pl.ds(pl.multiple_of(index * short, short), short), :]
+        return full_grads.at[part - 1, pl.ds(pl.multiple_of(index * tall, tall), tall), :]
+
+    full_acts[pl.ds(pl.multiple_of(me * short, short), short), :] = act_basis_ref[...]
+    for k in range(chunks):
+        full_grads[k, pl.ds(pl.multiple_of(me * tall, tall), tall), :] = grad_basis_ref[
+            :, k * CHUNK : (k + 1) * CHUNK
+        ]
+
+    def item_z(item):
+        if item == 0:
+            return z
+        return z - item if item < NZ else z + (item - NZ + 1)
+
+    def present(item):
+        if item == 0:
+            return z >= 0
+        return z >= item if item < NZ else z + (item - NZ + 1) <= NZ - 1
+
+    def copy_up(part, item):
+        ref = shard(part, item_z(item), x, core)
+        return remote(ref, ref, g_send.at[part, item], g_recv.at[part, item + 1], above)
+
+    def copy_down(part, item):
+        new = NZ if item == 0 else item + 1
+        ref = shard(part, item_z(item), x, core)
+        return remote(ref, ref, g_send.at[part, 3 + new], g_recv.at[part, new], below)
+
+    def copy_beside(part, item):
+        ref = shard(part, item_z(item), x, core)
+        return remote(ref, ref, g_send.at[part, 10 + item], g_recv.at[part, 7 + item], beside)
+
+    def copy_sibling(part, item):
+        ref = shard(part, item_z(item), x, core)
+        return remote(ref, ref, g_send.at[part, 17 + item], g_recv.at[part, 14 + item], sibling)
+
+    def copy_sibling_far(part, item):
+        ref = shard(part, item_z(item), 1 - x, core)
+        return remote(ref, ref, g_send.at[part, 24 + item], g_recv.at[part, 21 + item], sibling)
+
+    def came(part, item, slot, zz, xx, cc):
+        ref = shard(part, zz, xx, cc)
+        remote(ref, ref, g_send.at[part, 0], g_recv.at[part, slot], sibling).wait_recv()
+
+    def goes_up(item):
+        return jnp.logical_and(present(item), z < NZ - 1)
+
+    def goes_down(item):
+        return jnp.logical_and(present(item), z > 0)
+
+    def pass_on(part, item):
+        @pl.when(present(item))
+        def _():
+            if item > 0:
+                came(part, item, item, item_z(item), x, core)
+            copy_beside(part, item).start()
+
+        if item < NZ - 1:
+            @pl.when(goes_up(item))
+            def _():
+                copy_up(part, item).start()
+
+        if item == 0 or NZ <= item < 2 * NZ - 2:
+            @pl.when(goes_down(item))
+            def _():
+                copy_down(part, item).start()
+
+        @pl.when(present(item))
+        def _():
+            copy_sibling(part, item).start()
+
+    def pass_far(part, item):
+        @pl.when(present(item))
+        def _():
+            came(part, item, 7 + item, item_z(item), 1 - x, core)
+            copy_sibling_far(part, item).start()
+
+    def hop(part, h):
+        for item in ((0,) if h == 0 else (h, NZ - 1 + h)):
+            pass_on(part, item)
+
+    def hop_far(part, h):
+        for item in ((0,) if h == 0 else (h, NZ - 1 + h)):
+            pass_far(part, item)
+
+    def gathered(part):
+        for item in range(2 * NZ - 1):
+            @pl.when(present(item))
+            def _():
+                came(part, item, 14 + item, item_z(item), x, 1 - core)
+                came(part, item, 21 + item, item_z(item), 1 - x, 1 - core)
+
+    def drain(part):
+        for item in range(2 * NZ - 1):
+            @pl.when(present(item))
+            def _():
+                copy_beside(part, item).wait_send()
+                copy_sibling(part, item).wait_send()
+                copy_sibling_far(part, item).wait_send()
+
+            if item < NZ - 1:
+                @pl.when(goes_up(item))
+                def _():
+                    copy_up(part, item).wait_send()
+
+            if item == 0 or NZ <= item < 2 * NZ - 2:
+                @pl.when(goes_down(item))
+                def _():
+                    copy_down(part, item).wait_send()
+
+    def route():
+        lane = lax.broadcasted_iota(jnp.int32, (128, 128), 1)
+        row = lax.broadcasted_iota(jnp.int32, (128, 128), 0)
+        earlier = (row < lane).astype(bf16)
+        lines = ids_ref.shape[0]
+        above_line = (
+            lax.broadcasted_iota(jnp.int32, (lines, lines), 1)
+            < lax.broadcasted_iota(jnp.int32, (lines, lines), 0)
+        ).astype(bf16)
+        slots = slots_of(acts_ref, grads_ref)
+        place = lax.broadcasted_iota(jnp.int32, (capacity, 128), 0).astype(f32)
+        spot = lax.broadcasted_iota(jnp.int32, (capacity, 128), 1) // slots
+        picks, tokens, scales, members = [], [], [], []
+        for expert in (1 - own, own):
+            hit = jnp.where(ids_ref[...] == expert, 1.0, 0.0)
+            inside = jnp.dot(hit.astype(bf16), earlier, preferred_element_type=f32)
+            each = jnp.broadcast_to(jnp.sum(hit, axis=1, keepdims=True), hit.shape)
+            before = jnp.dot(above_line, each.astype(bf16), preferred_element_type=f32)
+            key = jnp.where(hit > 0.5, inside + before, -1.0)
+            pieces = []
+            scale = jnp.zeros((capacity, 128), f32)
+            token = jnp.zeros((capacity, 128), jnp.int32)
+            for i in range(lines):
+                chosen = place == key[i : i + 1, :]
+                pieces.append(jnp.where(chosen, 1.0, 0.0).astype(bf16))
+                scale = scale + jnp.where(chosen, probs_ref[i : i + 1, :], 0.0)
+                token = token + jnp.where(chosen, spot + (i * (128 // slots) + 1), 0)
+            scales.append(jnp.sum(scale, axis=1, keepdims=True))
+            token = jnp.sum(token, axis=1, keepdims=True) - 1
+            wide = lax.broadcasted_iota(jnp.int32, (capacity, grads_ref.shape[0]), 1) == token
+            label = jnp.sum(jnp.where(wide, labels_ref[...] + 1, 0), axis=1, keepdims=True) - 1
+            member = lax.broadcasted_iota(jnp.int32, (capacity, 128), 1) == label
+            members.append(jnp.where(member, 1.0, 0.0).astype(bf16))
+            picks.append(jnp.concatenate(pieces, axis=1))
+            tokens.append(jnp.where(wide, 1.0, 0.0).astype(bf16))
+        a = jnp.dot(jnp.concatenate(picks, axis=0), acts_ref[...], preferred_element_type=f32)
+        g = jnp.dot(jnp.concatenate(tokens, axis=0), grads_ref[...], preferred_element_type=f32)
+        g = g * jnp.concatenate(scales, axis=0)
+        send_a[...] = a[:capacity].astype(bf16)
+        send_g[...] = g[:capacity].astype(bf16)
+        send_m[...] = members[0]
+        for copy in exchange():
+            copy.start()
+        rows_a[0] = a[capacity:].astype(bf16)
+        rows_g[0] = g[capacity:].astype(bf16)
+        rows_m[0] = members[1]
+
+    def exchange():
+        pairs = ((send_a, rows_a), (send_g, rows_g), (send_m, rows_m))
+        return [
+            remote(src, dst.at[1], y_send.at[n], y_recv.at[n], partner)
+            for n, (src, dst) in enumerate(pairs)
+        ]
+
+    def rotate_acts():
+        for copy in exchange():
+            copy.wait_recv()
+        rows = rows_a[...].reshape(2 * capacity, rows_a.shape[2])
+        rotated = jnp.dot(rows, full_acts[...], preferred_element_type=f32)
+        turned = rotated.T.astype(bf16)
+        mask = rows_m[...].reshape(2 * capacity, 128).astype(f32).T.astype(bf16)
+        for index in range(4 * NZ):
+            zz, xx, cc = index // 4, index // 2 % 2, index % 2
+            b = (cc * 2 + xx) * NZ + zz
+            part = turned[index * block : (index + 1) * block, :]
+            for j in range(EXAMPLES):
+                masked[b, j * block : (j + 1) * block, :] = part * mask[j : j + 1, :]
+
+    def core_copy(k):
+        return remote(core_out.at[k], core_in.at[k], r_send.at[k, 0], r_recv.at[k, 0], sibling)
+
+    def x_copy(k):
+        return remote(x_out.at[k], x_in.at[k], r_send.at[k, 1], r_recv.at[k, 1], beside)
+
+    def up_copy(k, b):
+        return remote(
+            up_out.at[k, b], up_in.at[k, b], r_send.at[k, 2 + b], r_recv.at[k, 2 + b], above
+        )
+
+    def down_copy(k, b):
+        return remote(
+            down_out.at[k, b], down_in.at[k, b], r_send.at[k, 6 + b], r_recv.at[k, 6 + b], below
+        )
+
+    def squares(k):
+        rows = rows_g[...].reshape(2 * capacity, rows_g.shape[2])
+        rotated = jnp.dot(rows, full_grads[k], preferred_element_type=f32).astype(bf16)
+
+        def total(b):
+            product = jnp.dot(masked[b], rotated, preferred_element_type=f32)
+            product = product * product
+            return product[:block] + product[block : 2 * block] + product[2 * block :]
+
+        @pl.loop(0, 2 * NZ)
+        def _(n):
+            core_out[k, n] = total((1 - core) * (2 * NZ) + n).astype(bf16)
+
+        core_copy(k).start()
+
+        @pl.loop(0, 2 * NZ)
+        def _(n):
+            acc[k, n] = total(core * (2 * NZ) + n)
+
+    def to_beside(k):
+        core_copy(k).wait_recv()
+        far, near = (1 - x) * NZ, x * NZ
+
+        @pl.loop(0, NZ)
+        def _(n):
+            x_out[k, n] = (acc[k, far + n] + core_in[k, far + n].astype(f32)).astype(bf16)
+
+        x_copy(k).start()
+
+        @pl.loop(0, NZ)
+        def _(n):
+            acc[k, near + n] = acc[k, near + n] + core_in[k, near + n].astype(f32)
+
+    def to_line(k):
+        x_copy(k).wait_recv()
+        near = x * NZ
+
+        @pl.loop(0, NZ)
+        def _(n):
+            acc[k, near + n] = acc[k, near + n] + x_in[k, n].astype(f32)
+
+        for b in range(NZ):
+            @pl.when(jnp.logical_and(z == 0, b > z))
+            def _():
+                up_out[k, b] = acc[k, near + b].astype(bf16)
+                up_copy(k, b).start()
+
+            @pl.when(jnp.logical_and(z == NZ - 1, b < z))
+            def _():
+                down_out[k, b] = acc[k, near + b].astype(bf16)
+                down_copy(k, b).start()
+
+    def along(k):
+        near = x * NZ
+
+        def up(b):
+            @pl.when(jnp.logical_and(z > 0, b > z))
+            def _():
+                up_copy(k, b).wait_recv()
+                up_out[k, b] = (acc[k, near + b] + up_in[k, b].astype(f32)).astype(bf16)
+                up_copy(k, b).start()
+
+        def down(b):
+            @pl.when(jnp.logical_and(z < NZ - 1, b < z))
+            def _():
+                down_copy(k, b).wait_recv()
+                down_out[k, b] = (acc[k, near + b] + down_in[k, b].astype(f32)).astype(bf16)
+                down_copy(k, b).start()
+
+        for b in range(NZ):
+            up(NZ - 1 - b)
+            down(b)
+
+    def finish(k):
+        near = x * NZ
+        columns = slice(k * CHUNK, (k + 1) * CHUNK)
+        out_ref[:, columns] = acc[k, near + z]
+        for b in range(NZ):
+            @pl.when(jnp.logical_and(z > 0, z == b))
+            def _():
+                up_copy(k, b).wait_recv()
+                out_ref[:, columns] = out_ref[:, columns] + up_in[k, b].astype(f32)
+
+            @pl.when(jnp.logical_and(z < NZ - 1, z == b))
+            def _():
+                down_copy(k, b).wait_recv()
+                out_ref[:, columns] = out_ref[:, columns] + down_in[k, b].astype(f32)
+
+        out_ref[:, columns] = out_ref[:, columns] * (1.0 / (EXAMPLES * 4 * NZ))
+
+    def drain_sums(k):
+        core_copy(k).wait_send()
+        x_copy(k).wait_send()
+        for b in range(NZ):
+            @pl.when(jnp.logical_and(z < NZ - 1, b > z))
+            def _():
+                up_copy(k, b).wait_send()
+
+            @pl.when(jnp.logical_and(z > 0, b < z))
+            def _():
+                down_copy(k, b).wait_send()
+
+    parts = chunks + 1
+    AHEAD = 1
+    for part in range(AHEAD):
+        hop(part, 0)
+    for step in range(parts + 9):
+        if step + AHEAD < parts:
+            hop(step + AHEAD, 0)
+        if step == 0:
+            route()
+        for h in range(1, NZ):
+            if 0 <= step - h < parts:
+                hop(step - h, h)
+        for h in range(NZ):
+            if 0 <= step - h - 1 < parts:
+                hop_far(step - h - 1, h)
+        if 0 <= step - NZ < parts:
+            gathered(step - NZ)
+            if step == NZ:
+                rotate_acts()
+            else:
+                squares(step - NZ - 1)
+        if 0 <= step - NZ - 2 < chunks:
+            to_beside(step - NZ - 2)
+        if 0 <= step - NZ - 3 < chunks:
+            to_line(step - NZ - 3)
+        if 0 <= step - NZ - 4 < chunks:
+            along(step - NZ - 4)
+        if 0 <= step - NZ - 5 < chunks:
+            finish(step - NZ - 5)
+    for copy in exchange():
+        copy.wait_send()
+    for part in range(parts):
+        drain(part)
+    for k in range(chunks):
+        drain_sums(k)
+
+
+def slots_of(acts_ref, grads_ref):
+    return acts_ref.shape[0] // grads_ref.shape[0]
+
+
+def fused(acts, grads, probs, expert_ids, example_ids, act_basis, grad_basis):
+    tokens, slots, hidden = acts.shape
+    model = grads.shape[1]
+    capacity = tokens // 4
+    chunks = model // CHUNK
+    block = hidden // (4 * NZ)
+    bf16, f32 = jnp.bfloat16, jnp.float32
+    vm = pl.BlockSpec(memory_space=pltpu.VMEM)
+    dma = pltpu.SemaphoreType.DMA
+    result = pl.pallas_call(
+        kernel,
+        out_shape=jax.ShapeDtypeStruct((block, model), f32),
+        in_specs=[vm] * 7,
+        out_specs=vm,
+        scratch_shapes=[
+            pltpu.VMEM((hidden, hidden), bf16),
+            pltpu.VMEM((chunks, model, CHUNK), bf16),
+            pltpu.VMEM((capacity, hidden), bf16),
+            pltpu.VMEM((capacity, model), bf16),
+            pltpu.VMEM((capacity, 128), bf16),
+            pltpu.VMEM((2, capacity, hidden), bf16),
+            pltpu.VMEM((2, capacity, model), bf16),
+            pltpu.VMEM((2, capacity, 128), bf16),
+            pltpu.VMEM((4 * NZ, EXAMPLES * block, 2 * capacity), bf16),
+            pltpu.VMEM((chunks, 2 * NZ, block, CHUNK), f32),
+            pltpu.VMEM((chunks, 2 * NZ, block, CHUNK), bf16),
+            pltpu.VMEM((chunks, 2 * NZ, block, CHUNK), bf16),
+            pltpu.VMEM((chunks, NZ, block, CHUNK), bf16),
+            pltpu.VMEM((chunks, NZ, block, CHUNK), bf16),
+            pltpu.VMEM((chunks, NZ, block, CHUNK), bf16),
+            pltpu.VMEM((chunks, NZ, block, CHUNK), bf16),
+            pltpu.VMEM((chunks, NZ, block, CHUNK), bf16),
+            pltpu.VMEM((chunks, NZ, block, CHUNK), bf16),
+            dma((3,)),
+            dma((3,)),
+            dma((chunks + 1, 31)),
+            dma((chunks + 1, 28)),
+            dma((chunks, 10)),
+            dma((chunks, 10)),
+        ],
+        compiler_params=pltpu.CompilerParams(
+            collective_id=0, has_side_effects=True, vmem_limit_bytes=56 * 2**20
+        ),
+        cost_estimate=pl.CostEstimate(
+            flops=6 * 10**9, bytes_accessed=8 * 2**20, transcendentals=0
+        ),
+    )(
+        expert_ids.reshape(-1, 128),
+        probs.reshape(-1, 128),
+        example_ids,
+        acts.reshape(tokens * slots, hidden),
+        grads,
+        act_basis[0],
+        grad_basis[0],
+    )
+    return result[None]
+
+
 def solution(mesh):
+    small = mesh.shape["dp"] == 4 * NZ and mesh.shape["expert"] == 2
     return jax.shard_map(
-        body,
+        fused if small else body,
         mesh=mesh,
         in_specs=(
             P(("dp", "expert"), None, None),

time: 252 us -> 122 us (0.48)
  waiting for transfers between devices: 197 us -> 0 us
  Pallas kernels: 0 us -> 117 us
  between operations: 13.3 us -> 0.03 us
  starting transfers between devices: 11.3 us -> 0 us
  matrix products: 10.5 us -> 0 us
  other arithmetic: 8.3 us -> 0 us
  local copies, waits for them, and re-layouts: 11.3 us -> 4.93 us
    pallas_call x0 -> x1, Pallas kernels: none -> 117 us  [fused(): pl.pallas_call(kernel, out_shape=jax.ShapeDtypeStruct((block, model), f32...]
    reduce_scatter x1 -> x0, waiting for transfers between devices: 103 us -> none  [body(): result = lax.psum_scatter(totals, 'dp', scatter_dimension=0, tiled=True)]
    all_gather x2 -> x0, waiting for transfers between devices: 88.1 us -> none  [the longest x1 73.3 us: body(): lax.all_gather(basis_grads, 'dp', axis=0, tiled=True)]
    all_to_all x3 -> x0, starting transfers between devices: 11.2 us -> none  [the longest x1 4.23 us: body(): lax.all_to_all(send_member, 'expert', split_axis=0, concat_axis=0, tiled=...]
    dot_general x6 -> x0, matrix products: 10.5 us -> none  [the longest x1 4.63 us: body(): jnp.dot(routed_grads, full_grads, preferred_element_type=jnp.float32)]
    gather x9 -> x0, local copies, waits for them, and re-layouts: 9.37 us -> none  [the longest x1 3.77 us: route_block(): activity.reshape(count_tok * count_slot, activity.shape[-1])[flat_index]]
    mul x3 -> x0, other arithmetic: 4.97 us -> none  [the longest x1 4.15 us: body(): totals = jnp.concatenate(pieces, axis=0) * scale]
    all_to_all x3 -> x0, waiting for transfers between devices: 4.62 us -> none  [the longest x1 4.61 us: body(): lax.all_to_all(send_acts, 'expert', split_axis=0, concat_axis=0, tiled=True)]
  transfers between devices with their start and end apart: 6 -> 0, of which waited for: 4 -> 0; matrix products, arithmetic and copies ran while one was open for 7% -> 0% of each run, Pallas kernels for 0% -> 0%
where the time goes in v1:
time: 122 us
  Pallas kernels  117 us (96%)
  local copies, waits for them, and re-layouts  4.93 us (4%)
    pallas_call x1, Pallas kernels, fused(): pl.pallas_call(kernel, out_shape=jax.ShapeDtypeStruct((block, model), f32...  117 us
    unnamed x3, local copies, waits for them, and re-layouts  3.51 us

profile of v1, /device:TPU:0, one launch (start us, length us, event | category | flops | bytes accessed | tf_op | source)
XLA Modules:
  0.0 122.2 jit_solution(13045419450249109904)
XLA Ops:
  0.0 0.8 copy.11
  0.8 0.7 reshape.10.probs_ref
  1.5 0.8 copy.10
  2.4 0.7 reshape.9.ids_ref
  3.1 117.2 %shard_map.73 = f32[64,2048]{1,0:T(8,128)} custom-call(s32[16,128]{1,0:T(8,128)} %reshape.9.ids_ref, f32[16,128]{1,0:T(8,128)} %reshape.10.probs_ref, s32[1,256]{1,0:T(1,128)} %labels_ref.1, bf16[2048,1024]{1,0:T(8,128)(2,1)} %bitcast.5, bf16[256,2048]{1,0:T(8,128)(2,1)} %grads_ref.1, bf16[64,1024]{1,0:T(8,128)(2,1)} %bitcast.7, bf16[128,2048]{1,0:T(8,128)(2,1)} %bitcast.6), custom_call_target="tpu_custom_call" | custom-call | flops 6000000000 | bytes 8388608 | tf_op jit(solution)/shard_map/pallas_call | solution.py:489
  120.3 1.9 %copy.13 = f32[1,64,2048]{2,1,0:T(8,128)} copy(f32[1,64,2048]{2,1,0:T(8,128)} %bitcast.4) | data formatting | bytes 1048576

commit v2 on v1

--- a/solution.py
+++ b/solution.py
@@ -88,14 +88,14 @@
 
 
 NZ = 4
-CHUNK = 512
+CHUNK = 256
 
 
 def kernel(
     ids_ref, probs_ref, labels_ref, acts_ref, grads_ref, act_basis_ref, grad_basis_ref, out_ref,
     full_acts, full_grads, send_a, send_g, send_m, rows_a, rows_g, rows_m, masked,
-    acc, core_out, core_in, x_out, x_in, up_out, up_in, down_out, down_in,
-    y_send, y_recv, g_send, g_recv, r_send, r_recv,
+    acc, core_out, core_in, up_out, up_in, down_out, down_in, last_out, last_in,
+    y_send, y_recv, x_send, x_recv, g_send, g_recv, r_send, r_recv,
 ):
     me = lax.axis_index("dp")
     own = lax.axis_index("expert")
@@ -137,17 +137,28 @@
             device_id=target, device_id_type=pl.DeviceIdType.MESH,
         )
 
+    half = grad_basis_ref.shape[1] // 2
+
     def shard(part, zz, xx, cc):
-        index = (zz * 2 + xx) * 2 + cc
         if part == 0:
+            index = (zz * 2 + xx) * 2 + cc
             return full_acts.at[pl.ds(pl.multiple_of(index * short, short), short), :]
-        return full_grads.at[part - 1, pl.ds(pl.multiple_of(index * tall, tall), tall), :]
-
-    full_acts[pl.ds(pl.multiple_of(me * short, short), short), :] = act_basis_ref[...]
-    for k in range(chunks):
-        full_grads[k, pl.ds(pl.multiple_of(me * tall, tall), tall), :] = grad_basis_ref[
-            :, k * CHUNK : (k + 1) * CHUNK
-        ]
+        index = cc * NZ + zz
+        return full_grads.at[part - 1, pl.ds(pl.multiple_of(index * 2 * tall, tall), 2 * tall), :]
+
+    mine = pl.ds(pl.multiple_of(((core * NZ + z) * 2 + x) * tall, tall), tall)
+    theirs = pl.ds(pl.multiple_of(((core * NZ + z) * 2 + 1 - x) * tall, tall), tall)
+
+    def halves(k):
+        offset = pl.multiple_of((1 - x) * half + k * CHUNK, CHUNK)
+        return remote(
+            grad_basis_ref.at[:, pl.ds(offset, CHUNK)], full_grads.at[k, mine, :],
+            g_send.at[k + 1, 10], g_recv.at[k + 1, 7], beside,
+        )
+
+    def halves_came(k):
+        ref = full_grads.at[k, theirs, :]
+        remote(ref, ref, g_send.at[k + 1, 10], g_recv.at[k + 1, 7], beside).wait_recv()
 
     def item_z(item):
         if item == 0:
@@ -195,7 +206,10 @@
         def _():
             if item > 0:
                 came(part, item, item, item_z(item), x, core)
-            copy_beside(part, item).start()
+            elif part > 0:
+                halves_came(part - 1)
+            if part == 0:
+                copy_beside(part, item).start()
 
         if item < NZ - 1:
             @pl.when(goes_up(item))
@@ -230,15 +244,19 @@
             @pl.when(present(item))
             def _():
                 came(part, item, 14 + item, item_z(item), x, 1 - core)
-                came(part, item, 21 + item, item_z(item), 1 - x, 1 - core)
+                if part == 0:
+                    came(part, item, 21 + item, item_z(item), 1 - x, 1 - core)
 
     def drain(part):
         for item in range(2 * NZ - 1):
             @pl.when(present(item))
             def _():
-                copy_beside(part, item).wait_send()
                 copy_sibling(part, item).wait_send()
-                copy_sibling_far(part, item).wait_send()
+                if part == 0:
+                    copy_beside(part, item).wait_send()
+                    copy_sibling_far(part, item).wait_send()
+                elif item == 0:
+                    halves(part - 1).wait_send()
 
             if item < NZ - 1:
                 @pl.when(goes_up(item))
@@ -251,51 +269,60 @@
                     copy_down(part, item).wait_send()
 
     def route():
-        lane = lax.broadcasted_iota(jnp.int32, (128, 128), 1)
-        row = lax.broadcasted_iota(jnp.int32, (128, 128), 0)
-        earlier = (row < lane).astype(bf16)
-        lines = ids_ref.shape[0]
-        above_line = (
-            lax.broadcasted_iota(jnp.int32, (lines, lines), 1)
-            < lax.broadcasted_iota(jnp.int32, (lines, lines), 0)
-        ).astype(bf16)
-        slots = slots_of(acts_ref, grads_ref)
-        place = lax.broadcasted_iota(jnp.int32, (capacity, 128), 0).astype(f32)
-        spot = lax.broadcasted_iota(jnp.int32, (capacity, 128), 1) // slots
-        picks, tokens, scales, members = [], [], [], []
+        tokens, slots = ids_ref.shape[1], ids_ref.shape[0]
+
+        def iota(rows, columns, dim):
+            return lax.broadcasted_iota(jnp.int32, (rows, columns), dim)
+
+        def ones(mask):
+            return jnp.where(mask, 1.0, 0.0).astype(bf16)
+
+        earlier = ones(iota(tokens, tokens, 0) < iota(tokens, tokens, 1))
+        spread = ones(iota(tokens, tokens * slots, 0) == iota(tokens, tokens * slots, 1) // slots)
+        slot = iota(slots, tokens * slots, 1) % slots == iota(slots, tokens * slots, 0)
+        place = iota(capacity, tokens, 0).astype(f32)
+        picks, chosen, scales, members = [], [], [], []
         for expert in (1 - own, own):
             hit = jnp.where(ids_ref[...] == expert, 1.0, 0.0)
-            inside = jnp.dot(hit.astype(bf16), earlier, preferred_element_type=f32)
-            each = jnp.broadcast_to(jnp.sum(hit, axis=1, keepdims=True), hit.shape)
-            before = jnp.dot(above_line, each.astype(bf16), preferred_element_type=f32)
-            key = jnp.where(hit > 0.5, inside + before, -1.0)
-            pieces = []
-            scale = jnp.zeros((capacity, 128), f32)
-            token = jnp.zeros((capacity, 128), jnp.int32)
-            for i in range(lines):
-                chosen = place == key[i : i + 1, :]
-                pieces.append(jnp.where(chosen, 1.0, 0.0).astype(bf16))
-                scale = scale + jnp.where(chosen, probs_ref[i : i + 1, :], 0.0)
-                token = token + jnp.where(chosen, spot + (i * (128 // slots) + 1), 0)
-            scales.append(jnp.sum(scale, axis=1, keepdims=True))
-            token = jnp.sum(token, axis=1, keepdims=True) - 1
-            wide = lax.broadcasted_iota(jnp.int32, (capacity, grads_ref.shape[0]), 1) == token
-            label = jnp.sum(jnp.where(wide, labels_ref[...] + 1, 0), axis=1, keepdims=True) - 1
-            member = lax.broadcasted_iota(jnp.int32, (capacity, 128), 1) == label
-            members.append(jnp.where(member, 1.0, 0.0).astype(bf16))
-            picks.append(jnp.concatenate(pieces, axis=1))
-            tokens.append(jnp.where(wide, 1.0, 0.0).astype(bf16))
+            named = jnp.sum(hit, axis=0, keepdims=True)
+            rank = jnp.dot(
+                jnp.broadcast_to(named, hit.shape).astype(bf16), earlier,
+                preferred_element_type=f32,
+            )
+            key = jnp.where(named > 0.5, rank[:1], -1.0)
+            table = place == key
+            weight = jnp.sum(hit * probs_ref[...], axis=0, keepdims=True)
+            scales.append(jnp.sum(jnp.where(table, weight, 0.0), axis=1, keepdims=True))
+            label = jnp.sum(jnp.where(table, labels_ref[...] + 1, 0), axis=1, keepdims=True) - 1
+            members.append(ones(iota(capacity, 128, 1) == label))
+            flat = jnp.dot(hit.astype(bf16), spread, preferred_element_type=f32)
+            flat = jnp.sum(jnp.where(slot, flat, 0.0), axis=0, keepdims=True)
+            wide = jnp.dot(ones(table), spread, preferred_element_type=f32)
+            picks.append((wide * flat).astype(bf16))
+            chosen.append(ones(table))
         a = jnp.dot(jnp.concatenate(picks, axis=0), acts_ref[...], preferred_element_type=f32)
-        g = jnp.dot(jnp.concatenate(tokens, axis=0), grads_ref[...], preferred_element_type=f32)
-        g = g * jnp.concatenate(scales, axis=0)
+        g = jnp.dot(jnp.concatenate(chosen, axis=0), grads_ref[...], preferred_element_type=f32)
+        g = (g * jnp.concatenate(scales, axis=0)).astype(bf16)
+        g = jnp.concatenate(
+            [
+                g[:, index * tall : (index + 1) * tall]
+                for index in [
+                    (zz * 2 + xx) * 2 + cc
+                    for cc in range(2) for zz in range(NZ) for xx in range(2)
+                ]
+            ],
+            axis=1,
+        )
         send_a[...] = a[:capacity].astype(bf16)
-        send_g[...] = g[:capacity].astype(bf16)
+        send_g[...] = g[:capacity]
         send_m[...] = members[0]
         for copy in exchange():
             copy.start()
         rows_a[0] = a[capacity:].astype(bf16)
-        rows_g[0] = g[capacity:].astype(bf16)
+        rows_g[0] = g[capacity:]
         rows_m[0] = members[1]
+        for copy in exchange_x(0):
+            copy.start()
 
     def exchange():
         pairs = ((send_a, rows_a), (send_g, rows_g), (send_m, rows_m))
@@ -304,25 +331,43 @@
             for n, (src, dst) in enumerate(pairs)
         ]
 
+    def exchange_x(which):
+        return [
+            remote(
+                ref.at[which], ref.at[2 + which],
+                x_send.at[which, n], x_recv.at[which, n], beside,
+            )
+            for n, ref in enumerate((rows_a, rows_g, rows_m))
+        ]
+
+    def exchange_on():
+        for copy, later in zip(exchange(), exchange_x(1)):
+            copy.wait_recv()
+            later.start()
+
     def rotate_acts():
-        for copy in exchange():
-            copy.wait_recv()
-        rows = rows_a[...].reshape(2 * capacity, rows_a.shape[2])
+        for which in range(2):
+            for copy in exchange_x(which):
+                copy.wait_recv()
+        rows = rows_a[...].reshape(4 * capacity, rows_a.shape[2])
         rotated = jnp.dot(rows, full_acts[...], preferred_element_type=f32)
         turned = rotated.T.astype(bf16)
-        mask = rows_m[...].reshape(2 * capacity, 128).astype(f32).T.astype(bf16)
-        for index in range(4 * NZ):
-            zz, xx, cc = index // 4, index // 2 % 2, index % 2
-            b = (cc * 2 + xx) * NZ + zz
-            part = turned[index * block : (index + 1) * block, :]
-            for j in range(EXAMPLES):
-                masked[b, j * block : (j + 1) * block, :] = part * mask[j : j + 1, :]
+        for g in range(2):
+            mask = rows_m[2 * g : 2 * g + 2].reshape(2 * capacity, 128)
+            mask = mask.astype(f32).T.astype(bf16)
+            side = turned[:, g * 2 * capacity : (g + 1) * 2 * capacity]
+            for index in range(4 * NZ):
+                zz, xx, cc = index // 4, index // 2 % 2, index % 2
+                piece = side[index * block : (index + 1) * block, :]
+                for j in range(EXAMPLES):
+                    start = (j * 2 + xx) * block
+                    masked[g, cc * NZ + zz, start : start + block, :] = piece * mask[j : j + 1, :]
 
     def core_copy(k):
         return remote(core_out.at[k], core_in.at[k], r_send.at[k, 0], r_recv.at[k, 0], sibling)
 
-    def x_copy(k):
-        return remote(x_out.at[k], x_in.at[k], r_send.at[k, 1], r_recv.at[k, 1], beside)
+    def last_copy(k):
+        return remote(last_out.at[k], last_in.at[k], r_send.at[k, 1], r_recv.at[k, 1], beside)
 
     def up_copy(k, b):
         return remote(
@@ -335,72 +380,60 @@
         )
 
     def squares(k):
-        rows = rows_g[...].reshape(2 * capacity, rows_g.shape[2])
+        rows = rows_g[...].reshape(4 * capacity, rows_g.shape[2])
         rotated = jnp.dot(rows, full_grads[k], preferred_element_type=f32).astype(bf16)
+        groups = [rotated[g * 2 * capacity : (g + 1) * 2 * capacity] for g in range(2)]
 
         def total(b):
-            product = jnp.dot(masked[b], rotated, preferred_element_type=f32)
-            product = product * product
-            return product[:block] + product[block : 2 * block] + product[2 * block :]
-
-        @pl.loop(0, 2 * NZ)
-        def _(n):
-            core_out[k, n] = total((1 - core) * (2 * NZ) + n).astype(bf16)
-
-        core_copy(k).start()
-
-        @pl.loop(0, 2 * NZ)
-        def _(n):
-            acc[k, n] = total(core * (2 * NZ) + n)
-
-    def to_beside(k):
-        core_copy(k).wait_recv()
-        far, near = (1 - x) * NZ, x * NZ
+            result = None
+            for g in range(2):
+                product = jnp.dot(masked[g, b], groups[g], preferred_element_type=f32)
+                for j in range(EXAMPLES):
+                    one = product[j * 2 * block : (j + 1) * 2 * block]
+                    result = one * one if result is None else result + one * one
+            return result
 
         @pl.loop(0, NZ)
         def _(n):
-            x_out[k, n] = (acc[k, far + n] + core_in[k, far + n].astype(f32)).astype(bf16)
-
-        x_copy(k).start()
+            core_out[k, n] = total((1 - core) * NZ + n).astype(bf16)
+
+        core_copy(k).start()
 
         @pl.loop(0, NZ)
         def _(n):
-            acc[k, near + n] = acc[k, near + n] + core_in[k, near + n].astype(f32)
+            acc[k, n] = total(core * NZ + n)
 
     def to_line(k):
-        x_copy(k).wait_recv()
-        near = x * NZ
+        core_copy(k).wait_recv()
 
         @pl.loop(0, NZ)
         def _(n):
-            acc[k, near + n] = acc[k, near + n] + x_in[k, n].astype(f32)
+            acc[k, n] = acc[k, n] + core_in[k, n].astype(f32)
 
         for b in range(NZ):
             @pl.when(jnp.logical_and(z == 0, b > z))
             def _():
-                up_out[k, b] = acc[k, near + b].astype(bf16)
+                up_out[k, b] = acc[k, b].astype(bf16)
                 up_copy(k, b).start()
 
             @pl.when(jnp.logical_and(z == NZ - 1, b < z))
             def _():
-                down_out[k, b] = acc[k, near + b].astype(bf16)
+                down_out[k, b] = acc[k, b].astype(bf16)
                 down_copy(k, b).start()
 
     def along(k):
-        near = x * NZ
-
         def up(b):
             @pl.when(jnp.logical_and(z > 0, b > z))
             def _():
                 up_copy(k, b).wait_recv()
-                up_out[k, b] = (acc[k, near + b] + up_in[k, b].astype(f32)).astype(bf16)
+                up_out[k, b] = (acc[k, b] + up_in[k, b].astype(f32)).astype(bf16)
                 up_copy(k, b).start()
 
         def down(b):
             @pl.when(jnp.logical_and(z < NZ - 1, b < z))
             def _():
                 down_copy(k, b).wait_recv()
-                down_out[k, b] = (acc[k, near + b] + down_in[k, b].astype(f32)).astype(bf16)
+                down_out[k, b] = (acc[k, b] + down_in[k, b].astype(f32)).astype(bf16)
                 down_copy(k, b).start()
 
         for b in range(NZ):
@@ -408,25 +441,33 @@
             down(b)
 
     def finish(k):
-        near = x * NZ
-        columns = slice(k * CHUNK, (k + 1) * CHUNK)
-        out_ref[:, columns] = acc[k, near + z]
         for b in range(NZ):
             @pl.when(jnp.logical_and(z > 0, z == b))
             def _():
                 up_copy(k, b).wait_recv()
-                out_ref[:, columns] = out_ref[:, columns] + up_in[k, b].astype(f32)
+                acc[k, b] = acc[k, b] + up_in[k, b].astype(f32)
 
             @pl.when(jnp.logical_and(z < NZ - 1, z == b))
             def _():
                 down_copy(k, b).wait_recv()
-                out_ref[:, columns] = out_ref[:, columns] + down_in[k, b].astype(f32)
-
-        out_ref[:, columns] = out_ref[:, columns] * (1.0 / (EXAMPLES * 4 * NZ))
+                acc[k, b] = acc[k, b] + down_in[k, b].astype(f32)
+
+        scale = 1.0 / (EXAMPLES * 4 * NZ)
+        near = pl.ds(pl.multiple_of(x * block, block), block)
+        far = pl.ds(pl.multiple_of((1 - x) * block, block), block)
+        last_out[k] = acc[k, z, far, :] * scale
+        last_copy(k).start()
+        columns = pl.ds(pl.multiple_of(x * half + k * CHUNK, CHUNK), CHUNK)
+        out_ref[:, columns] = acc[k, z, near, :] * scale
+
+    def place_last(k):
+        last_copy(k).wait_recv()
+        columns = pl.ds(pl.multiple_of((1 - x) * half + k * CHUNK, CHUNK), CHUNK)
+        out_ref[:, columns] = last_in[k]
 
     def drain_sums(k):
         core_copy(k).wait_send()
-        x_copy(k).wait_send()
+        last_copy(k).wait_send()
         for b in range(NZ):
             @pl.when(jnp.logical_and(z < NZ - 1, b > z))
             def _():
@@ -437,20 +478,28 @@
                 down_copy(k, b).wait_send()
 
     parts = chunks + 1
-    AHEAD = 1
-    for part in range(AHEAD):
-        hop(part, 0)
-    for step in range(parts + 9):
-        if step + AHEAD < parts:
-            hop(step + AHEAD, 0)
+    ahead = 2
+    full_acts[pl.ds(pl.multiple_of(me * short, short), short), :] = act_basis_ref[...]
+    hop(0, 0)
+    for k in range(chunks):
+        halves(k).start()
+    for k in range(chunks):
+        offset = pl.multiple_of(x * half + k * CHUNK, CHUNK)
+        full_grads[k, mine, :] = grad_basis_ref[:, pl.ds(offset, CHUNK)]
+    hop(1, 0)
+    for step in range(parts + NZ + 4):
+        if step + ahead < parts:
+            hop(step + ahead, 0)
         if step == 0:
             route()
         for h in range(1, NZ):
             if 0 <= step - h < parts:
                 hop(step - h, h)
+        if step == 1:
+            exchange_on()
         for h in range(NZ):
-            if 0 <= step - h - 1 < parts:
-                hop_far(step - h - 1, h)
+            if step - h - 1 == 0:
+                hop_far(0, h)
         if 0 <= step - NZ < parts:
             gathered(step - NZ)
             if step == NZ:
@@ -458,13 +507,16 @@
             else:
                 squares(step - NZ - 1)
         if 0 <= step - NZ - 2 < chunks:
-            to_beside(step - NZ - 2)
+            to_line(step - NZ - 2)
         if 0 <= step - NZ - 3 < chunks:
-            to_line(step - NZ - 3)
+            along(step - NZ - 3)
+        if 0 <= step - NZ - 3 < chunks:
+            finish(step - NZ - 3)
         if 0 <= step - NZ - 4 < chunks:
-            along(step - NZ - 4)
-        if 0 <= step - NZ - 5 < chunks:
-            finish(step - NZ - 5)
+            place_last(step - NZ - 4)
+    for which in range(2):
+        for copy in exchange_x(which):
+            copy.wait_send()
     for copy in exchange():
         copy.wait_send()
     for part in range(parts):
@@ -473,15 +525,11 @@
         drain_sums(k)
 
 
-def slots_of(acts_ref, grads_ref):
-    return acts_ref.shape[0] // grads_ref.shape[0]
-
-
 def fused(acts, grads, probs, expert_ids, example_ids, act_basis, grad_basis):
     tokens, slots, hidden = acts.shape
     model = grads.shape[1]
     capacity = tokens // 4
-    chunks = model // CHUNK
+    chunks = model // 2 // CHUNK
     block = hidden // (4 * NZ)
     bf16, f32 = jnp.bfloat16, jnp.float32
     vm = pl.BlockSpec(memory_space=pltpu.VMEM)
@@ -497,21 +545,23 @@
             pltpu.VMEM((capacity, hidden), bf16),
             pltpu.VMEM((capacity, model), bf16),
             pltpu.VMEM((capacity, 128), bf16),
-            pltpu.VMEM((2, capacity, hidden), bf16),
-            pltpu.VMEM((2, capacity, model), bf16),
-            pltpu.VMEM((2, capacity, 128), bf16),
-            pltpu.VMEM((4 * NZ, EXAMPLES * block, 2 * capacity), bf16),
-            pltpu.VMEM((chunks, 2 * NZ, block, CHUNK), f32),
-            pltpu.VMEM((chunks, 2 * NZ, block, CHUNK), bf16),
-            pltpu.VMEM((chunks, 2 * NZ, block, CHUNK), bf16),
-            pltpu.VMEM((chunks, NZ, block, CHUNK), bf16),
-            pltpu.VMEM((chunks, NZ, block, CHUNK), bf16),
-            pltpu.VMEM((chunks, NZ, block, CHUNK), bf16),
-            pltpu.VMEM((chunks, NZ, block, CHUNK), bf16),
-            pltpu.VMEM((chunks, NZ, block, CHUNK), bf16),
-            pltpu.VMEM((chunks, NZ, block, CHUNK), bf16),
+            pltpu.VMEM((4, capacity, hidden), bf16),
+            pltpu.VMEM((4, capacity, model), bf16),
+            pltpu.VMEM((4, capacity, 128), bf16),
+            pltpu.VMEM((2, 2 * NZ, EXAMPLES * 2 * block, 2 * capacity), bf16),
+            pltpu.VMEM((chunks, NZ, 2 * block, CHUNK), f32),
+            pltpu.VMEM((chunks, NZ, 2 * block, CHUNK), bf16),
+            pltpu.VMEM((chunks, NZ, 2 * block, CHUNK), bf16),
+            pltpu.VMEM((chunks, NZ, 2 * block, CHUNK), bf16),
+            pltpu.VMEM((chunks, NZ, 2 * block, CHUNK), bf16),
+            pltpu.VMEM((chunks, NZ, 2 * block, CHUNK), bf16),
+            pltpu.VMEM((chunks, NZ, 2 * block, CHUNK), bf16),
+            pltpu.VMEM((chunks, block, CHUNK), f32),
+            pltpu.VMEM((chunks, block, CHUNK), f32),
             dma((3,)),
             dma((3,)),
+            dma((2, 3)),
+            dma((2, 3)),
             dma((chunks + 1, 31)),
             dma((chunks + 1, 28)),
             dma((chunks, 10)),
@@ -524,8 +574,8 @@
             flops=6 * 10**9, bytes_accessed=8 * 2**20, transcendentals=0
         ),
     )(
-        expert_ids.reshape(-1, 128),
-        probs.reshape(-1, 128),
+        expert_ids.T,
+        probs.T,
         example_ids,
         acts.reshape(tokens * slots, hidden),
         grads,

time: 122 us -> 109 us (0.89)
  Pallas kernels: 117 us -> 107 us
  local copies, waits for them, and re-layouts: 4.93 us -> 1.87 us
    pallas_call x1, Pallas kernels: 117 us -> 107 us  [fused(): pl.pallas_call(kernel, out_shape=jax.ShapeDtypeStruct((block, model), f32...]
    unnamed x3 -> x1, local copies, waits for them, and re-layouts: 3.51 us -> 1.87 us
    reshape x2 -> x0, local copies, waits for them, and re-layouts: 1.42 us -> none  [the longest x1 0.71 us: fused(): expert_ids.reshape(-1, 128)]
where the time goes in v2:
time: 109 us
  Pallas kernels  107 us (98%)
  local copies, waits for them, and re-layouts  1.87 us (2%)
    pallas_call x1, Pallas kernels, fused(): pl.pallas_call(kernel, out_shape=jax.ShapeDtypeStruct((block, model), f32...  107 us

profile of v2, /device:TPU:0, one launch (start us, length us, event | category | flops | bytes accessed | tf_op | source)
XLA Modules:
  0.0 109.2 jit_solution(12258615208358100057)
XLA Ops:
  0.0 107.4 %shard_map.73 = f32[64,2048]{1,0:T(8,128)} custom-call(s32[8,256]{1,0:T(8,128)} %bitcast.10, f32[8,256]{1,0:T(8,128)} %bitcast.11, s32[1,256]{1,0:T(1,128)} %labels_ref.1, bf16[2048,1024]{1,0:T(8,128)(2,1)} %bitcast.7, bf16[256,2048]{1,0:T(8,128)(2,1)} %grads_ref.1, bf16[64,1024]{1,0:T(8,128)(2,1)} %bitcast.9, bf16[128,2048]{1,0:T(8,128)(2,1)} %bitcast.8), custom_call_target="tpu_custom_call" | custom-call | flops 6000000000 | bytes 8388608 | tf_op jit(solution)/shard_map/pallas_call | solution.py:537
  107.4 1.9 %copy.9 = f32[1,64,2048]{2,1,0:T(8,128)} copy(f32[1,64,2048]{2,1,0:T(8,128)} %bitcast.6) | data formatting | bytes 1048576

commit v3 on v2

--- a/solution.py
+++ b/solution.py
@@ -117,7 +117,7 @@
     partner = {"expert": 1 - own}
 
     barrier = pltpu.get_barrier_semaphore()
-    for target in (sibling, beside, partner):
+    for target in (beside, partner):
         pl.semaphore_signal(barrier, inc=1, device_id=target, device_id_type=pl.DeviceIdType.MESH)
 
     @pl.when(z < NZ - 1)
@@ -129,7 +129,13 @@
         pl.semaphore_signal(barrier, inc=1, device_id=below, device_id_type=pl.DeviceIdType.MESH)
 
     ends = (z == 0).astype(jnp.int32) + (z == NZ - 1).astype(jnp.int32)
-    pl.semaphore_wait(barrier, 5 - ends)
+    pl.semaphore_wait(barrier, 4 - ends + core)
+    pl.semaphore_signal(barrier, inc=1, device_id=sibling, device_id_type=pl.DeviceIdType.MESH)
+
+    def meet_sibling():
+        @pl.when(core == 0)
+        def _():
+            pl.semaphore_wait(barrier, 1)
 
     def remote(src, dst, ssem, rsem, target):
         return pltpu.make_async_remote_copy(
@@ -221,9 +227,11 @@
             def _():
                 copy_down(part, item).start()
 
-        @pl.when(present(item))
-        def _():
-            copy_sibling(part, item).start()
+    def share(part, h):
+        for item in ((0,) if h == 0 else (h, NZ - 1 + h)):
+            @pl.when(present(item))
+            def _():
+                copy_sibling(part, item).start()
 
     def pass_far(part, item):
         @pl.when(present(item))
@@ -487,19 +495,29 @@
         offset = pl.multiple_of(x * half + k * CHUNK, CHUNK)
         full_grads[k, mine, :] = grad_basis_ref[:, pl.ds(offset, CHUNK)]
     hop(1, 0)
+    met = 2
+    waiting = [(0, 0), (1, 0)]
     for step in range(parts + NZ + 4):
         if step + ahead < parts:
             hop(step + ahead, 0)
+            waiting.append((step + ahead, 0))
         if step == 0:
             route()
         for h in range(1, NZ):
             if 0 <= step - h < parts:
                 hop(step - h, h)
+                waiting.append((step - h, h))
         if step == 1:
             exchange_on()
-        for h in range(NZ):
-            if step - h - 1 == 0:
-                hop_far(0, h)
+        if step == met:
+            meet_sibling()
+        if step >= met:
+            for part, h in waiting:
+                share(part, h)
+            waiting = []
+            for h in range(NZ):
+                if step - h - 1 == 0 or (step == met and h < step - 1):
+                    hop_far(0, h)
         if 0 <= step - NZ < parts:
             gathered(step - NZ)
             if step == NZ:

time: 109 us -> 113 us (1.037)
  Pallas kernels: 107 us -> 111 us
    pallas_call x1, Pallas kernels: 107 us -> 111 us  [fused(): pl.pallas_call(kernel, out_shape=jax.ShapeDtypeStruct((block, model), f32...]
where the time goes in v3:
time: 113 us
  Pallas kernels  111 us (98%)
  local copies, waits for them, and re-layouts  1.87 us (2%)
    pallas_call x1, Pallas kernels, fused(): pl.pallas_call(kernel, out_shape=jax.ShapeDtypeStruct((block, model), f32...  111 us

profile of v3, /device:TPU:0, one launch (start us, length us, event | category | flops | bytes accessed | tf_op | source)
XLA Modules:
  0.0 112.6 jit_solution(4320317268566445218)
XLA Ops:
  0.0 110.7 %shard_map.73 = f32[64,2048]{1,0:T(8,128)} custom-call(s32[8,256]{1,0:T(8,128)} %bitcast.10, f32[8,256]{1,0:T(8,128)} %bitcast.11, s32[1,256]{1,0:T(1,128)} %labels_ref.1, bf16[2048,1024]{1,0:T(8,128)(2,1)} %bitcast.7, bf16[256,2048]{1,0:T(8,128)(2,1)} %grads_ref.1, bf16[64,1024]{1,0:T(8,128)(2,1)} %bitcast.9, bf16[128,2048]{1,0:T(8,128)(2,1)} %bitcast.8), custom_call_target="tpu_custom_call" | custom-call | flops 6000000000 | bytes 8388608 | tf_op jit(solution)/shard_map/pallas_call | solution.py:555
  110.7 1.9 %copy.9 = f32[1,64,2048]{2,1,0:T(8,128)} copy(f32[1,64,2048]{2,1,0:T(8,128)} %bitcast.6) | data formatting | bytes 1048576
